TPU v7x, 256 devices: a whole 4x4x8 slice. The times are simulated.
256 devices in a mesh: row: 32 (over x, y, core), col: 8 (over z).
Axes of the slice: x: 4, y: 4, z: 8, core: 2. Of those that a mesh axis runs over, the one named last changes fastest.
Arguments:
- lower_earlier: bfloat16 [16, 96, 512, 512], P('col', 'row'), may hold values from -0.0546875 to 0.0546875
- lower_current: bfloat16 [16, 3, 512, 512], P('col', None, 'row'), may hold values from -0.25 to 0.25
- inverse_diagonal: bfloat16 [3, 512, 512], replicated, may hold values from -1 to 2, as said below
- solved_earlier: bfloat16 [96, 512, 1024], P('row'), may hold values from -6 to 6
- statistics: float32 [512, 16, 1024], P('row', 'col'), may hold values from -6 to 6
Outputs:
- reduced_statistics: float32 [512, 16, 1024], P('row', 'col')
- solved_blocks: bfloat16 [3, 512, 1024], P(None, 'row')
Inputs may be any that keep to these rules, and one draw needn't show every extreme that they name: `inverse_diagonal`: each block is lower triangular with diagonal entries between 0.5 and 2 and entries below the diagonal of magnitude under one.
All inputs are finite; a program needn't handle non-finite values.
Results may differ from a plain program's by a relative error of at most 0.008.
Values may be sent and summed in bfloat16 or wider, within the bound.
A program may use at most 64 MiB of HBM per device.

v0:
```python
import jax
import jax.numpy as jnp
from jax import lax
from jax.sharding import PartitionSpec as P

STEPS = 3


def broadcast(block, axis, source):
    block = jnp.where(lax.axis_index(axis) == source, block, jnp.zeros_like(block))
    return lax.psum(block, axis)


def earlier_term(panel, solved_earlier):
    return jnp.einsum("abnq,bqm->nam", panel, solved_earlier, preferred_element_type=jnp.float32)


def per_device(lower_earlier, lower_current, inverse_diagonal, solved_earlier, statistics):
    row_share = lower_current.shape[2]
    window_rows = statistics.shape[1]
    col_count = lax.axis_size("col")
    row_index = lax.axis_index("row")
    column_index = lax.axis_index("col")
    earlier_sum = lax.psum_scatter(
        earlier_term(lower_earlier, solved_earlier), "row", scatter_dimension=0, tiled=True
    )
    reduced = statistics - earlier_sum
    solutions = []
    for k in range(STEPS):
        leading = reduced[:, 0, :]
        for j in range(k):
            leading = leading - jnp.dot(
                lower_current[0, j], solutions[j], preferred_element_type=jnp.float32
            )
        pivotal = leading.astype(jnp.bfloat16)
        portion = broadcast(pivotal, "col", k)
        whole_block = lax.all_gather(portion, "row", axis=0, tiled=True)
        solution = jnp.dot(
            inverse_diagonal[k], whole_block, preferred_element_type=jnp.float32
        ).astype(jnp.bfloat16)
        solutions.append(solution)
    position = column_index + col_count * jnp.arange(window_rows, dtype=jnp.int32)
    updated = reduced
    for k in range(STEPS):
        product = jnp.einsum(
            "acq,qm->cam", lower_current[:, k], solutions[k], preferred_element_type=jnp.float32
        )
        active = (position > k)[None, :, None]
        updated = updated - jnp.where(active, product, jnp.float32(0.0))
    stacked = jnp.stack(solutions)
    own_rows = lax.dynamic_slice_in_dim(stacked, row_index * row_share, row_share, 1)
    return (updated, own_rows)


def solution(mesh):
    placed = (
        P("col", "row", None, None),
        P("col", None, "row", None),
        P(),
        P("row", None, None),
        P("row", "col", None),
    )
    return jax.shard_map(
        per_device,
        mesh=mesh,
        in_specs=placed,
        out_specs=(P("row", "col", None), P(None, "row", None)),
        check_vma=False,
    )
```

profile of v0, /device:TPU:32, one launch (start us, length us, event | category | flops | bytes accessed | tf_op | source)
XLA Modules:
  0.0 393.0 jit_solution(17975914423485741709)
XLA Ops:
  7.2 0.0 all-reduce.3.cloned.1.call-start
  7.2 1.8 copy-done
  9.1 7.0 %fusion.2 = f32[512,2,1024]{0,2,1:T(8,128)} fusion(bf16[2,3,512,512]{3,2,1,0:T(8,128)(2,1)S(1)} %copy-done, bf16[3,512,1024]{2,1,0:T(8,128)(2,1)} %param.8), kind=kOutput, calls=%fused_computation.5 | convolution fusion | flops 3221225472 | bytes 10485760 | tf_op jit(solution)/shard_map/abnq,bqm->nam/dot_general | solution.py:15
  16.0 7.3 %copy.21 = f32[512,2,1024]{2,1,0:T(2,128)} copy(f32[512,2,1024]{0,2,1:T(8,128)} %fusion.2) | data formatting | bytes 8388608 | tf_op jit(solution)/shard_map/abnq,bqm->nam/transpose | solution.py:15
  23.4 0.0 all-gather.4.cloned.1.call-start
  23.5 0.6 copy-done.7
  24.1 0.6 dynamic-slice
  25.3 122.6 %all-reduce.3.cloned.1.call-done = f32[512,2,1024]{2,1,0:T(2,128)} async-done(((f32[512,2,1024]{2,1,0:T(2,128)}), f32[512,2,1024]{2,1,0:T(2,128)}) %all-reduce.3.cloned.1.call-update) | async-done | bytes 4194320
  147.9 0.9 constant_dynamic-slice_fusion
  148.9 0.1 copy_subtract_fusion
  149.0 29.0 %psum.21 = bf16[16,1024]{1,0:T(8,128)(2,1)} all-reduce(bf16[16,1024]{1,0:T(8,128)(2,1)S(1)} %fusion.27), channel_id=1, replica_groups=mesh['row'=32,'col'=8] {'col'}, use_global_device_ids=true, to_apply=%region_1.2 | all-reduce | flops 16384 | bytes 65536 | tf_op jit(solution)/shard_map/psum | solution.py:11
  177.9 0.0 all-gather.4.cloned.1.call-update
  177.9 0.0 all-gather.6.cloned.1.call-start
  178.0 46.5 %all-gather.4.cloned.1.call-done = bf16[512,1024]{1,0:T(8,128)(2,1)} async-done(((bf16[16,1024]{1,0:T(8,128)(2,1)}), bf16[512,1024]{1,0:T(8,128)(2,1)}) %all-gather.4.cloned.1.call-update) | async-done | bytes 1048592 | tf_op jit(solution)/shard_map/all_gather | solution.py:37
  224.5 2.1 convolution_convert_fusion.2
  226.6 1.0 copy-done.1
  227.5 0.3 convert_select_fusion
  227.8 28.9 %psum.22 = bf16[16,1024]{1,0:T(8,128)(2,1)} all-reduce(bf16[16,1024]{1,0:T(8,128)(2,1)S(1)} %get-tuple-element.6), channel_id=1, replica_groups=mesh['row'=32,'col'=8] {'col'}, use_global_device_ids=true, to_apply=%region_2.3 | all-reduce | flops 16384 | bytes 65536 | tf_op jit(solution)/shard_map/psum | solution.py:11
  256.8 0.0 all-gather.8.cloned.1.call-start
  256.8 46.5 %all-gather.6.cloned.1.call-done = bf16[512,1024]{1,0:T(8,128)(2,1)} async-done(((bf16[16,1024]{1,0:T(8,128)(2,1)}), bf16[512,1024]{1,0:T(8,128)(2,1)}) %all-gather.6.cloned.1.call-update) | async-done | bytes 1048592 | tf_op jit(solution)/shard_map/all_gather | solution.py:37
  303.3 2.1 convolution_convert_fusion.1
  305.4 1.0 copy-done.3
  306.4 0.3 fusion.14
  306.7 28.9 %psum.23 = bf16[16,1024]{1,0:T(8,128)(2,1)} all-reduce(bf16[16,1024]{1,0:T(8,128)(2,1)S(1)} %fusion.14), channel_id=1, replica_groups=mesh['row'=32,'col'=8] {'col'}, use_global_device_ids=true, to_apply=%region_3.4 | all-reduce | flops 16384 | bytes 65536 | tf_op jit(solution)/shard_map/psum | solution.py:11
  335.6 0.0 all-gather.8.cloned.1.call-update
  335.7 1.5 fusion.6
  337.2 45.0 %all-gather.8.cloned.1.call-done = bf16[512,1024]{1,0:T(8,128)(2,1)} async-done(((bf16[16,1024]{1,0:T(8,128)(2,1)}), bf16[512,1024]{1,0:T(8,128)(2,1)}) %all-gather.8.cloned.1.call-update) | async-done | bytes 1048592 | tf_op jit(solution)/shard_map/all_gather | solution.py:37
  382.2 2.2 convolution_convert_fusion
  384.5 0.3 fusion.5
  384.8 0.3 fusion.10
  385.1 0.8 copy.30
  385.8 0.6 fusion.25
  (17 shorter events, 0.1 us)
Async XLA Ops:
  7.2 1.9 copy-start
  7.2 140.8 %all-reduce.3.cloned.1.call-start = ((), (), s32[]{:S(2)}) async-start(), calls=%async_computation.3 | async-start | bytes 8388608
  23.4 0.7 copy-start.7
  23.4 125.5 %copy-start.6 = (f32[16,2,1024]{2,1,0:T(2,128)S(1)}, f32[16,2,1024]{2,1,0:T(2,128)}, u32[]{:S(2)}) copy-start(f32[16,2,1024]{2,1,0:T(2,128)} %param.9) | copy-start | bytes 393220
  23.4 204.2 %copy-start.5 = (bf16[2,3,16,512]{3,2,1,0:T(8,128)(2,1)S(1)}, bf16[2,3,16,512]{3,2,1,0:T(8,128)(2,1)}, u32[]{:S(2)}) copy-start(bf16[2,3,16,512]{3,2,1,0:T(8,128)(2,1)} %param.6) | copy-start | bytes 294916
  23.4 201.0 %all-gather.4.cloned.1.call-start = ((), (), s32[]{:S(2)}) async-start(), calls=%async_computation | async-start | bytes 1081344 | tf_op jit(solution)/shard_map/all_gather | solution.py:37
  177.9 125.4 %all-gather.6.cloned.1.call-start = ((), (), s32[]{:S(2)}) async-start(), calls=%async_computation.1 | async-start | bytes 1081344 | tf_op jit(solution)/shard_map/all_gather | solution.py:37
  226.6 1.0 copy-start.1
  256.8 125.5 %all-gather.8.cloned.1.call-start = ((), (), s32[]{:S(2)}) async-start(), calls=%async_computation.2 | async-start | bytes 1081344 | tf_op jit(solution)/shard_map/all_gather | solution.py:37
  305.4 1.0 copy-start.3
  382.2 2.5 copy-start.2
  382.2 3.6 copy-start.4
Sparse Core Ops, SparseCore 0:
  23.5 124.3 all-reduce.2
  178.1 46.3 all-gather.3
  256.9 46.3 all-gather.5
  335.8 46.3 all-gather.7
where the time goes:
time: 395 us; the launch traced here: 393 us
  waiting for transfers between devices  261 us (66%)
  blocking collectives  86.8 us (22%)
  matrix products  16 us (4%)
  between operations  14.6 us (4%)
  local copies, waits for them, and re-layouts  14 us (4%)
    all_gather x3, waiting for transfers between devices, per_device(): whole_block = lax.all_gather(portion, 'row', axis=0, tiled=True)  138 us
    unnamed x5, waiting for transfers between devices  123 us
    psum x3, blocking collectives, broadcast(): return lax.psum(block, axis)  86.8 us
  transfers between devices with their start and end apart: 4, of which 4 were waited for; matrix products, arithmetic and copies ran while one was open for 1% of the time, Pallas kernels for 0%

commit v1 on v0

v1 whole, which is shorter than its diff:
```python
import jax
import jax.numpy as jnp
from jax import lax
from jax.experimental import pallas as pl
from jax.experimental.pallas import tpu as pltpu
from jax.sharding import PartitionSpec as P

MESH = pl.DeviceIdType.MESH
F32 = jnp.float32
BF16 = jnp.bfloat16
SIDE = 4
CHIPS = 16
PLANES = 8


def lanes_low(shape):
    return lax.broadcasted_iota(jnp.int32, shape, len(shape) - 1) < 64


def swap(value):
    return pltpu.roll(value, 64, 1)


def dot(a, b):
    return jnp.dot(a, b, preferred_element_type=F32)


def wait_bytes(ref, sem):
    pltpu.make_async_copy(ref, ref, sem).wait()


def kernel(
    le, s, lc, inv, stat, upd, sol,
    sv, lev, invv, statv, csend, crecv, acc, rssend, rsrecv, lg, stage, rz, q, xs, xg, usend, ug, red,
    load_sem, own_sem, c_ssem, c_rsem, rs_ssem, rs_rsem, l_ssem, l_rsem, st_ssem, st_rsem,
    rz_ssem, rz_rsem, z_ssem, z_rsem, q_ssem, q_rsem, x_ssem, x_rsem, u_ssem, u_rsem,
):
    row = lax.axis_index("row")
    z = lax.axis_index("col")
    c = lax.rem(row, 2)
    p = row // 2
    x = p // SIDE
    y = lax.rem(p, SIDE)
    sib = (row + 1 - 2 * c, z)
    low = lanes_low((128, 128))

    def peer(d):
        px = lax.rem(x + d // SIDE, SIDE)
        py = lax.rem(y + lax.rem(d, SIDE), SIDE)
        return px * SIDE + py

    def remote(src, dst, ssem, rsem, device):
        return pltpu.make_async_remote_copy(
            src_ref=src, dst_ref=dst, send_sem=ssem, recv_sem=rsem, device_id=device, device_id_type=MESH
        )

    loads = []
    for a, slot in ((0, 0), (0, 1), (1, 0), (1, 1)):
        half = (1 - c) if slot == 0 else c
        loads.append(pltpu.make_async_copy(le.at[a, :, :, half], lev.at[a, slot], load_sem.at[2 * a + slot]))
    s_loads = [pltpu.make_async_copy(s.at[b], sv.at[b], load_sem.at[4 + b]) for b in range(3)]
    inv_load = pltpu.make_async_copy(inv, invv, load_sem.at[7])
    stat_load = pltpu.make_async_copy(stat, statv, load_sem.at[8])
    loads[0].start()
    for cp in s_loads:
        cp.start()
    for cp in loads[1:] + [stat_load, inv_load]:
        cp.start()

    barrier = pltpu.get_barrier_semaphore()

    def greet(d, carry):
        pl.semaphore_signal(barrier, inc=1, device_id=(2 * peer(d) + c, z), device_id_type=MESH)
        return carry

    def greet_z(d, carry):
        pl.semaphore_signal(barrier, inc=1, device_id=(row, lax.rem(z + d, PLANES)), device_id_type=MESH)
        return carry

    pl.semaphore_signal(barrier, inc=1, device_id=sib, device_id_type=MESH)
    lax.fori_loop(1, CHIPS, greet, 0)
    lax.fori_loop(1, PLANES, greet_z, 0)

    def product(a, slot, columns):
        total = None
        for b in range(3):
            term = dot(lev[a, slot, b].reshape(256, 512), sv[b, :, columns])
            total = term if total is None else total + term
        return total

    def block_columns(i):
        return pl.ds(pl.multiple_of(lax.rem(x + i, SIDE) * 256, 256), 256)

    def c_copy(a, i):
        return remote(csend.at[a, i], crecv.at[a, i], c_ssem.at[a, i], c_rsem.at[a, i], sib)

    def other_block(a, i):
        csend[a, i] = product(a, 0, block_columns(i)).astype(BF16)

    def own_block(a, i):
        columns = block_columns(i)
        total = product(a, 1, columns)
        c_copy(a, i).wait_recv()
        acc[...] = total + crecv[a, i].astype(F32)
        mine = pl.ds(pl.multiple_of(16 * p, 16), 16)
        acc[mine, :] = acc[mine, :] - statv[:, a, columns]
        for t in range(2):
            lo = acc[0:128, 128 * t : 128 * t + 128]
            hi = acc[128:256, 128 * t : 128 * t + 128]
            rssend[a, SIDE * i + 2 * t] = jnp.where(low, lo, swap(hi)).astype(BF16)
            rssend[a, SIDE * i + 2 * t + 1] = jnp.where(low, swap(lo), hi).astype(BF16)

        def send(j):
            py = lax.rem(y + j, SIDE)
            px = lax.rem(x + i, SIDE)
            remote(
                rssend.at[a, SIDE * i + py],
                rsrecv.at[a, SIDE * i + j],
                rs_ssem.at[a],
                rs_rsem.at[a],
                (2 * (px * SIDE + py) + c, z),
            ).start()

        for j in range(SIDE):
            if j == 0:
                pl.when(i > 0)(lambda: send(0))
            else:
                send(j)

    def both_halves(a, first):
        def other(i, carry):
            other_block(a, i)
            c_copy(a, i).start()
            return carry

        def own(i, carry):
            own_block(a, i)
            return carry

        lax.fori_loop(first, SIDE, other, 0)
        loads[2 * a + 1].wait()
        lax.fori_loop(0, SIDE, own, 0)

    loads[0].wait()
    for cp in s_loads:
        cp.wait()
    other_block(0, 0)
    pl.semaphore_wait(barrier, CHIPS - 1 + 1 + PLANES - 1)
    c_copy(0, 0).start()

    stage_copies = (
        remote(lc.at[0, pl.ds(0, 1)], stage.at[pl.ds(0, 1)], st_ssem, st_rsem.at[0], (row, 0)),
        remote(lc.at[0, pl.ds(0, 2)], stage.at[pl.ds(1, 2)], st_ssem, st_rsem.at[1], (row, 0)),
    )
    for t in range(2):
        pl.when(z == t + 1)(lambda: stage_copies[t].start())
    stat_load.wait()
    both_halves(0, 1)

    def gather(part, src):
        def send(d, carry):
            remote(
                src, lg.at[pl.ds(3 * part, 3), p], l_ssem.at[part], l_rsem.at[part], (2 * peer(d) + c, z)
            ).start()
            return carry

        lax.fori_loop(1, CHIPS, send, 0)
        pltpu.make_async_copy(src, lg.at[pl.ds(3 * part, 3), p], own_sem.at[part]).start()

    def gather_wait(part):
        wait_bytes(lg.at[pl.ds(3 * part, 3), pl.ds(0, CHIPS - 1)], l_rsem.at[part])
        wait_bytes(stage, own_sem.at[part])

    @pl.when(z != 0)
    def _():
        gather(0, lc.at[0])

    @pl.when(z == 0)
    def _():
        for t in range(2):
            stage_copies[t].wait_recv()
        gather(0, stage)

    gather(1, lc.at[1])

    loads[2].wait()
    both_halves(1, 0)
    inv_load.wait()

    def reduced(a):
        wait_bytes(rsrecv.at[a, pl.ds(1, CHIPS - 1)], rs_rsem.at[a])
        total = rssend[a, y].astype(F32)
        for d in range(1, CHIPS):
            total = total + rsrecv[a, d].astype(F32)
        red[a] = -total

    reduced(0)

    rz[2] = red[0]
    rz_copies = [remote(rz.at[2], rz.at[t], rz_ssem, rz_rsem.at[t], (row, 0)) for t in range(2)]
    for t in range(2):
        pl.when(z == t + 1)(lambda: rz_copies[t].start())

    def applied(block, k):
        panel = lg[block].reshape(256, 512)
        solved = xs[k].reshape(256, 128)
        first = dot(panel[:, 0:256], solved)
        second = dot(panel[:, 256:512], solved)
        return jnp.where(low, first[0:128], second[128:256]) + swap(
            jnp.where(low, first[128:256], second[0:128])
        )

    def update(k):
        red[1] = red[1] - applied(3 + k, k)

        @pl.when(z > k)
        def _():
            red[0] = red[0] - applied(k, k)

    def x_send(k):
        def send(d, carry):
            target = peer(d)
            remote(
                xs.at[k, lax.rem(target, 8), c], xg.at[k, p], x_ssem.at[k], x_rsem.at[k], (2 * target + c, z)
            ).start()
            return carry

        lax.fori_loop(1, CHIPS, send, 0)
        xg[k, p] = xs[k, lax.rem(p, 8), c]

    def z_copy(k, d):
        return remote(
            q.at[k, :, c], q.at[k, :, c], z_ssem.at[k, d - 1], z_rsem.at[k], (row, lax.rem(z + d, PLANES))
        )

    def sib_copy(k):
        return remote(q.at[k, :, c], q.at[k, :, c], q_ssem.at[k], q_rsem.at[k], sib)

    def sib_back(k):
        return remote(q.at[k, :, 1 - c], q.at[k, :, 1 - c], q_ssem.at[k], q_rsem.at[k], sib)

    for k in range(3):

        @pl.when(z == 0)
        def _():
            if k == 0:
                pivotal = red[0]
            elif k == 1:
                gather_wait(0)
                pivotal = -applied(0, 0)
                rz_copies[0].wait_recv()
                pivotal = rz[0] + pivotal
            else:
                pivotal = -applied(1, 0) - applied(2, 1)
                rz_copies[1].wait_recv()
                pivotal = rz[1] + pivotal
            q[k, :, c] = pivotal.astype(BF16).reshape(8, 16, 128)
            sib_copy(k).start()
            for d in range(1, PLANES):
                z_copy(k, d).start()

        @pl.when(z != 0)
        def _():
            if k == 1:
                gather_wait(0)
                gather_wait(1)
                reduced(1)
            if k > 0:
                x_send(k - 1)
                update(k - 1)
            z_copy(k, 1).wait_recv()
            sib_copy(k).start()

        sib_back(k).wait_recv()
        pivotal = q[k].reshape(256, 128)
        left = dot(invv[k, :, 0:256], pivotal)
        right = dot(invv[k, 256:512, 256:512], pivotal)
        low_x = lanes_low((256, 128))
        solved = jnp.where(low_x, left[0:256], right + swap(left[256:512]))
        xs[k] = solved.astype(BF16).reshape(8, 2, 16, 128)

    @pl.when(z == 0)
    def _():
        gather_wait(1)
        reduced(1)
        for k in range(2):
            x_send(k)
            update(k)

    @pl.when((z == 1) | (z == 2))
    def _():
        wait_bytes(rz.at[2], rz_ssem)

    update(2)
    first, second = red[0], red[1]
    usend[0:8] = jnp.where(low, first, swap(second)).reshape(8, 16, 128)
    usend[8:16] = jnp.where(low, swap(first), second).reshape(8, 16, 128)

    def u_send(d, carry):
        target = peer(d)
        remote(usend.at[target], ug.at[p], u_ssem, u_rsem, (2 * target + c, z)).start()
        return carry

    lax.fori_loop(1, CHIPS, u_send, 0)
    ug[p] = usend[p]
    x_send(2)

    low_t = lanes_low((16, 128))
    early = p < 8

    def solved_out(k):
        wait_bytes(xg.at[k, pl.ds(0, CHIPS - 1)], x_rsem.at[k])
        for t in range(8):
            even = xg[k, 2 * t].astype(F32)
            odd = xg[k, 2 * t + 1].astype(F32)
            value = jnp.where(
                early, jnp.where(low_t, even, swap(odd)), jnp.where(low_t, swap(even), odd)
            )
            sol[k, :, 128 * t : 128 * t + 128] = value.astype(BF16)

    solved_out(0)
    solved_out(1)
    wait_bytes(ug.at[pl.ds(0, CHIPS - 1)], u_rsem)
    for t in range(8):
        even, odd = ug[2 * t], ug[2 * t + 1]
        upd[0, :, 128 * t : 128 * t + 128] = jnp.where(low_t, even, swap(odd))
        upd[1, :, 128 * t : 128 * t + 128] = jnp.where(low_t, swap(even), odd)
    solved_out(2)

    for a in range(2):
        for i in range(SIDE):
            c_copy(a, i).wait_send()
        wait_bytes(rssend.at[a, pl.ds(0, CHIPS - 1)], rs_ssem.at[a])
        wait_bytes(lg.at[pl.ds(3 * a, 3), pl.ds(0, CHIPS - 1)], l_ssem.at[a])
    for t in range(2):
        pl.when(z == t + 1)(lambda: stage_copies[t].wait_send())
    for k in range(3):
        sib_copy(k).wait_send()
        wait_bytes(xg.at[k, pl.ds(0, CHIPS - 1)], x_ssem.at[k])

        @pl.when(z == 0)
        def _():
            for d in range(1, PLANES):
                z_copy(k, d).wait_send()

    wait_bytes(ug.at[pl.ds(0, CHIPS - 1)], u_ssem)


def per_device(lower_earlier, lower_current, inverse_diagonal, solved_earlier, statistics):
    dma = pltpu.SemaphoreType.DMA
    any_space = pl.BlockSpec(memory_space=pl.ANY)
    vmem = pl.BlockSpec(memory_space=pltpu.VMEM)
    upd, sol = pl.pallas_call(
        kernel,
        out_shape=(
            jax.ShapeDtypeStruct((2, 16, 1024), F32),
            jax.ShapeDtypeStruct((3, 16, 1024), BF16),
        ),
        in_specs=[any_space] * 5,
        out_specs=(vmem, vmem),
        scratch_shapes=[
            pltpu.VMEM((3, 512, 1024), BF16),
            pltpu.VMEM((2, 2, 3, 16, 16, 512), BF16),
            pltpu.VMEM((3, 512, 512), BF16),
            pltpu.VMEM((16, 2, 1024), F32),
            pltpu.VMEM((2, 4, 256, 256), BF16),
            pltpu.VMEM((2, 4, 256, 256), BF16),
            pltpu.VMEM((256, 256), F32),
            pltpu.VMEM((2, 16, 128, 128), BF16),
            pltpu.VMEM((2, 16, 128, 128), BF16),
            pltpu.VMEM((6, 16, 16, 512), BF16),
            pltpu.VMEM((3, 16, 512), BF16),
            pltpu.VMEM((3, 128, 128), F32),
            pltpu.VMEM((3, 8, 2, 16, 128), BF16),
            pltpu.VMEM((3, 8, 2, 16, 128), BF16),
            pltpu.VMEM((3, 16, 16, 128), BF16),
            pltpu.VMEM((16, 16, 128), F32),
            pltpu.VMEM((16, 16, 128), F32),
            pltpu.VMEM((2, 128, 128), F32),
            dma((9,)),
            dma((2,)),
            dma((2, 4)), dma((2, 4)),
            dma((2,)), dma((2,)),
            dma((2,)), dma((2,)),
            dma, dma((2,)),
            dma, dma((2,)),
            dma((3, 7)), dma((3,)),
            dma((3,)), dma((3,)),
            dma((3,)), dma((3,)),
            dma, dma,
        ],
        compiler_params=pltpu.CompilerParams(
            collective_id=0, has_side_effects=True, vmem_limit_bytes=56 * 1024 * 1024
        ),
        cost_estimate=pl.CostEstimate(flops=3400000000, bytes_accessed=9000000, transcendentals=0),
    )(
        lower_earlier.reshape(2, 3, 16, 2, 16, 512),
        solved_earlier,
        lower_current,
        inverse_diagonal,
        statistics,
    )
    return jnp.swapaxes(upd, 0, 1), sol


def solution(mesh):
    placed = (
        P("col", "row", None, None),
        P("col", None, "row", None),
        P(),
        P("row", None, None),
        P("row", "col", None),
    )
    return jax.shard_map(
        per_device,
        mesh=mesh,
        in_specs=placed,
        out_specs=(P("row", "col", None), P(None, "row", None)),
        check_vma=False,
    )
```

time: 395 us -> 58.9 us (0.15)
  waiting for transfers between devices: 261 us -> 0 us
  blocking collectives: 86.8 us -> 0 us
  Pallas kernels: 0 us -> 54.9 us
  matrix products: 16 us -> 0 us
  between operations: 14.6 us -> 0.64 us
  local copies, waits for them, and re-layouts: 14 us -> 3.2 us
    all_gather x3 -> x0, waiting for transfers between devices: 138 us -> none  [per_device(): whole_block = lax.all_gather(portion, 'row', axis=0, tiled=True)]
    unnamed x5 -> x0, waiting for transfers between devices: 123 us -> none
    psum x3 -> x0, blocking collectives: 86.8 us -> none  [broadcast(): return lax.psum(block, axis)]
    pallas_call x0 -> x1, Pallas kernels: none -> 54.9 us  [per_device(): pl.pallas_call(kernel, out_shape=(jax.ShapeDtypeStruct((2, 16, 1024), F32...]
    dot_general x9 -> x0, matrix products: 16 us -> none  [the longest x1 6.99 us: earlier_term(): jnp.einsum('abnq,bqm->nam', panel, solved_earlier, preferred_element_type...]
    transpose x1 -> x0, local copies, waits for them, and re-layouts: 7.33 us -> none  [earlier_term(): jnp.einsum('abnq,bqm->nam', panel, solved_earlier, preferred_element_type...]
  transfers between devices with their start and end apart: 4 -> 0, of which waited for: 4 -> 0; matrix products, arithmetic and copies ran while one was open for 1% -> 0% of each run, Pallas kernels for 0% -> 0%
where the time goes in v1:
time: 58.9 us; the launch traced here: 58.7 us
  Pallas kernels  54.9 us (93%)
  local copies, waits for them, and re-layouts  3.2 us (5%)
  between operations  0.64 us (1%)
    pallas_call x1, Pallas kernels, per_device(): pl.pallas_call(kernel, out_shape=(jax.ShapeDtypeStruct((2, 16, 1024), F32...  54.9 us
    unnamed x2, local copies, waits for them, and re-layouts  3.2 us

profile of v1, /device:TPU:32, one launch (start us, length us, event | category | flops | bytes accessed | tf_op | source)
XLA Modules:
  0.0 58.7 jit_solution(6695658630770805365)
XLA Ops:
  0.6 54.9 %shard_map.68 = (f32[2,16,1024]{2,1,0:T(8,128)}, bf16[3,16,1024]{2,1,0:T(8,128)(2,1)}) custom-call(bf16[2,3,16,2,16,512]{5,4,3,2,1,0:T(8,128)(2,1)} %bitcast.3, bf16[3,512,1024]{2,1,0:T(8,128)(2,1)} %s.1, bf16[2,3,16,512]{3,2,1,0:T(8,128)(2,1)} %lc.1, bf16[3,512,512]{2,1,0:T(8,128)(2,1)} %inv.1, f32[16,2,1024]{2,1,0:T(2,128)} %stat.1), custom_call_target="tpu_custom_call" | custom-call | flops 3400000000 | bytes 9000000 | tf_op jit(solution)/shard_map/pallas_call | solution.py:353
  55.5 1.7 %copy.7 = f32[16,2,1024]{2,1,0:T(2,128)} copy(f32[16,2,1024]{2,0,1:T(8,128)} %bitcast.2) | data formatting | bytes 262144
  57.2 1.5 %copy.9 = bf16[3,16,1024]{2,1,0:T(8,128)(2,1)} copy(bf16[3,16,1024]{2,1,0:T(8,128)(2,1)} %get-tuple-element.11) | data formatting | bytes 196608

commit v2 on v1

--- a/solution.py
+++ b/solution.py
@@ -31,8 +31,8 @@
 
 def kernel(
     le, s, lc, inv, stat, upd, sol,
-    sv, lev, invv, statv, csend, crecv, acc, rssend, rsrecv, lg, stage, rz, q, xs, xg, usend, ug, red,
-    load_sem, own_sem, c_ssem, c_rsem, rs_ssem, rs_rsem, l_ssem, l_rsem, st_ssem, st_rsem,
+    sv, lev, invv, statv, csend, crecv, acc, rssend, rsrecv, lg, rz, q, xs, xg, usend, ug, red,
+    load_sem, own_sem, c_ssem, c_rsem, rs_ssem, rs_rsem, l_ssem, l_rsem, f_ssem, f_rsem, ch_ssem,
     rz_ssem, rz_rsem, z_ssem, z_rsem, q_ssem, q_rsem, x_ssem, x_rsem, u_ssem, u_rsem,
 ):
     row = lax.axis_index("row")
@@ -48,6 +48,12 @@
         px = lax.rem(x + d // SIDE, SIDE)
         py = lax.rem(y + lax.rem(d, SIDE), SIDE)
         return px * SIDE + py
+
+    def x_peer(d):
+        return 2 * (lax.rem(x + d, SIDE) * SIDE + y) + c
+
+    def y_peer(d):
+        return 2 * (x * SIDE + lax.rem(y + d, SIDE)) + c
 
     def remote(src, dst, ssem, rsem, device):
         return pltpu.make_async_remote_copy(
@@ -73,13 +79,27 @@
         pl.semaphore_signal(barrier, inc=1, device_id=(2 * peer(d) + c, z), device_id_type=MESH)
         return carry
 
-    def greet_z(d, carry):
-        pl.semaphore_signal(barrier, inc=1, device_id=(row, lax.rem(z + d, PLANES)), device_id_type=MESH)
-        return carry
-
     pl.semaphore_signal(barrier, inc=1, device_id=sib, device_id_type=MESH)
     lax.fori_loop(1, CHIPS, greet, 0)
-    lax.fori_loop(1, PLANES, greet_z, 0)
+
+    @pl.when(z == 0)
+    def _():
+        for d in range(1, PLANES):
+            pl.semaphore_signal(barrier, inc=1, device_id=(row, d), device_id_type=MESH)
+        for t in range(1, 3):
+            for d in range(1, SIDE):
+                pl.semaphore_signal(barrier, inc=1, device_id=(x_peer(d), t), device_id_type=MESH)
+
+    @pl.when(z > 0)
+    def _():
+        pl.semaphore_signal(barrier, inc=1, device_id=(row, 0), device_id_type=MESH)
+
+    @pl.when((z == 1) | (z == 2))
+    def _():
+        for d in range(1, SIDE):
+            pl.semaphore_signal(barrier, inc=1, device_id=(x_peer(d), 0), device_id_type=MESH)
+
+    partners = CHIPS + jnp.where(z == 0, 7 + 6, jnp.where(z <= 2, 1 + 3, 1))
 
     def product(a, slot, columns):
         total = None
@@ -127,7 +147,7 @@
             else:
                 send(j)
 
-    def both_halves(a, first):
+    def both_halves(a, first, between=None):
         def other(i, carry):
             other_block(a, i)
             c_copy(a, i).start()
@@ -138,6 +158,8 @@
             return carry
 
         lax.fori_loop(first, SIDE, other, 0)
+        if between is not None:
+            between()
         loads[2 * a + 1].wait()
         lax.fori_loop(0, SIDE, own, 0)
 
@@ -145,46 +167,78 @@
     for cp in s_loads:
         cp.wait()
     other_block(0, 0)
-    pl.semaphore_wait(barrier, CHIPS - 1 + 1 + PLANES - 1)
+    pl.semaphore_wait(barrier, partners)
     c_copy(0, 0).start()
 
-    stage_copies = (
-        remote(lc.at[0, pl.ds(0, 1)], stage.at[pl.ds(0, 1)], st_ssem, st_rsem.at[0], (row, 0)),
-        remote(lc.at[0, pl.ds(0, 2)], stage.at[pl.ds(1, 2)], st_ssem, st_rsem.at[1], (row, 0)),
-    )
-    for t in range(2):
-        pl.when(z == t + 1)(lambda: stage_copies[t].start())
+    def near(part, device):
+        remote(lc.at[part], lg.at[pl.ds(3 * part, 3), x, y], l_ssem.at[part], l_rsem.at[part], device).start()
+
+    own_part = [pltpu.make_async_copy(lc.at[t], lg.at[pl.ds(3 * t, 3), x, y], own_sem.at[t]) for t in range(2)]
+
+    def chain_block(t, d):
+        span = pl.ds(t - 1, t)
+        return remote(
+            lc.at[0, pl.ds(0, t)], lg.at[span, x, y], ch_ssem.at[d], l_rsem.at[0], (x_peer(d), 0)
+        )
+
+    @pl.when(z != 0)
+    def _():
+        for d in range(1, SIDE):
+            near(0, (x_peer(d), z))
+        own_part[0].start()
+
+    for t in (1, 2):
+
+        @pl.when(z == t)
+        def _():
+            for d in range(SIDE):
+                chain_block(t, d).start()
+
+    for d in range(1, SIDE):
+        near(1, (y_peer(d), z))
+    own_part[1].start()
+
     stat_load.wait()
     both_halves(0, 1)
 
-    def gather(part, src):
-        def send(d, carry):
-            remote(
-                src, lg.at[pl.ds(3 * part, 3), p], l_ssem.at[part], l_rsem.at[part], (2 * peer(d) + c, z)
-            ).start()
-            return carry
-
-        lax.fori_loop(1, CHIPS, send, 0)
-        pltpu.make_async_copy(src, lg.at[pl.ds(3 * part, 3), p], own_sem.at[part]).start()
+    def far_source(part):
+        return lg.at[pl.ds(0, 3), :, y] if part == 0 else lg.at[pl.ds(3, 3), x]
+
+    def far(part):
+        for d in range(1, SIDE):
+            device = (y_peer(d) if part == 0 else x_peer(d), z)
+            remote(far_source(part), far_source(part), f_ssem.at[part], f_rsem.at[part], device).start()
+
+    def three_near(part):
+        return lg.at[pl.ds(3 * part, 3), 0, pl.ds(0, 3)]
+
+    def three_far(part):
+        return lg.at[pl.ds(3 * part, 3), pl.ds(0, 3)]
+
+    def near_wait(part):
+        wait_bytes(three_near(part), l_rsem.at[part])
+        own_part[part].wait()
 
     def gather_wait(part):
-        wait_bytes(lg.at[pl.ds(3 * part, 3), pl.ds(0, CHIPS - 1)], l_rsem.at[part])
-        wait_bytes(stage, own_sem.at[part])
-
-    @pl.when(z != 0)
-    def _():
-        gather(0, lc.at[0])
+        wait_bytes(three_far(part), f_rsem.at[part])
+
+    def relay():
+        @pl.when(z != 0)
+        def _():
+            near_wait(0)
+            far(0)
+
+        near_wait(1)
+        far(1)
+
+    loads[2].wait()
+    both_halves(1, 0, relay)
 
     @pl.when(z == 0)
     def _():
-        for t in range(2):
-            stage_copies[t].wait_recv()
-        gather(0, stage)
-
-    gather(1, lc.at[1])
-
-    loads[2].wait()
-    both_halves(1, 0)
+        wait_bytes(far_source(0), l_rsem.at[0])
+        far(0)
+
     inv_load.wait()
 
     def reduced(a):
@@ -331,9 +385,20 @@
         for i in range(SIDE):
             c_copy(a, i).wait_send()
         wait_bytes(rssend.at[a, pl.ds(0, CHIPS - 1)], rs_ssem.at[a])
-        wait_bytes(lg.at[pl.ds(3 * a, 3), pl.ds(0, CHIPS - 1)], l_ssem.at[a])
-    for t in range(2):
-        pl.when(z == t + 1)(lambda: stage_copies[t].wait_send())
+        wait_bytes(three_far(a), f_ssem.at[a])
+
+    @pl.when(z != 0)
+    def _():
+        wait_bytes(three_near(0), l_ssem.at[0])
+
+    wait_bytes(three_near(1), l_ssem.at[1])
+    for t in (1, 2):
+
+        @pl.when(z == t)
+        def _():
+            for d in range(SIDE):
+                chain_block(t, d).wait_send()
+
     for k in range(3):
         sib_copy(k).wait_send()
         wait_bytes(xg.at[k, pl.ds(0, CHIPS - 1)], x_ssem.at[k])
@@ -368,8 +433,7 @@
             pltpu.VMEM((256, 256), F32),
             pltpu.VMEM((2, 16, 128, 128), BF16),
             pltpu.VMEM((2, 16, 128, 128), BF16),
-            pltpu.VMEM((6, 16, 16, 512), BF16),
-            pltpu.VMEM((3, 16, 512), BF16),
+            pltpu.VMEM((6, 4, 4, 16, 512), BF16),
             pltpu.VMEM((3, 128, 128), F32),
             pltpu.VMEM((3, 8, 2, 16, 128), BF16),
             pltpu.VMEM((3, 8, 2, 16, 128), BF16),
@@ -382,7 +446,8 @@
             dma((2, 4)), dma((2, 4)),
             dma((2,)), dma((2,)),
             dma((2,)), dma((2,)),
-            dma, dma((2,)),
+            dma((2,)), dma((2,)),
+            dma((4,)),
             dma, dma((2,)),
             dma((3, 7)), dma((3,)),
             dma((3,)), dma((3,)),

time: 58.9 us -> 51.1 us (0.87)
  the two profiles are of different devices: /device:TPU:32 before, /device:TPU:97 now
where the time goes in v2:
time: 51.1 us; the launch traced here: 51 us
  Pallas kernels  47.1 us (92%)
  local copies, waits for them, and re-layouts  3.2 us (6%)
  between operations  0.64 us (1%)
    pallas_call x1, Pallas kernels, per_device(): pl.pallas_call(kernel, out_shape=(jax.ShapeDtypeStruct((2, 16, 1024), F32...  47.1 us
    unnamed x2, local copies, waits for them, and re-layouts  3.2 us

profile of v2, /device:TPU:97, one launch (start us, length us, event | category | flops | bytes accessed | tf_op | source)
XLA Modules:
  0.0 51.0 jit_solution(1397326152821441287)
XLA Ops:
  0.6 47.1 %shard_map.68 = (f32[2,16,1024]{2,1,0:T(8,128)}, bf16[3,16,1024]{2,1,0:T(8,128)(2,1)}) custom-call(bf16[2,3,16,2,16,512]{5,4,3,2,1,0:T(8,128)(2,1)} %bitcast.3, bf16[3,512,1024]{2,1,0:T(8,128)(2,1)} %s.1, bf16[2,3,16,512]{3,2,1,0:T(8,128)(2,1)} %lc.1, bf16[3,512,512]{2,1,0:T(8,128)(2,1)} %inv.1, f32[16,2,1024]{2,1,0:T(2,128)} %stat.1), custom_call_target="tpu_custom_call" | custom-call | flops 3400000000 | bytes 9000000 | tf_op jit(solution)/shard_map/pallas_call | solution.py:418
  47.8 1.7 %copy.7 = f32[16,2,1024]{2,1,0:T(2,128)} copy(f32[16,2,1024]{2,0,1:T(8,128)} %bitcast.2) | data formatting | bytes 262144
  49.4 1.5 %copy.9 = bf16[3,16,1024]{2,1,0:T(8,128)(2,1)} copy(bf16[3,16,1024]{2,1,0:T(8,128)(2,1)} %get-tuple-element.11) | data formatting | bytes 196608

commit v3 on v2

--- a/solution.py
+++ b/solution.py
@@ -32,7 +32,7 @@
 def kernel(
     le, s, lc, inv, stat, upd, sol,
     sv, lev, invv, statv, csend, crecv, acc, rssend, rsrecv, lg, rz, q, xs, xg, usend, ug, red,
-    load_sem, own_sem, c_ssem, c_rsem, rs_ssem, rs_rsem, l_ssem, l_rsem, f_ssem, f_rsem, ch_ssem,
+    load_sem, own_sem, c_ssem, c_rsem, rs_ssem, rs_rsem, l_ssem, l_rsem, f_ssem, f_rsem, ch_ssem, ch_rsem, ready_sem,
     rz_ssem, rz_rsem, z_ssem, z_rsem, q_ssem, q_rsem, x_ssem, x_rsem, u_ssem, u_rsem,
 ):
     row = lax.axis_index("row")
@@ -79,27 +79,28 @@
         pl.semaphore_signal(barrier, inc=1, device_id=(2 * peer(d) + c, z), device_id_type=MESH)
         return carry
 
-    pl.semaphore_signal(barrier, inc=1, device_id=sib, device_id_type=MESH)
+    def signal(sem, device):
+        pl.semaphore_signal(sem, inc=1, device_id=device, device_id_type=MESH)
+
+    @pl.when(z == 0)
+    def _():
+        for d in (4, 3, 5, 6, 7, 2, 1):
+            signal(barrier, (row, d))
+        for t in (2, 1):
+            for d in (2, 1, 3):
+                signal(barrier, (x_peer(d), t))
+                signal(barrier, (y_peer(d), t))
+
+    @pl.when((z == 1) | (z == 2))
+    def _():
+        signal(barrier, (row, 0))
+        for d in (2, 1, 3):
+            signal(barrier, (x_peer(d), 0))
+            signal(barrier, (y_peer(d), 0))
+
     lax.fori_loop(1, CHIPS, greet, 0)
-
-    @pl.when(z == 0)
-    def _():
-        for d in range(1, PLANES):
-            pl.semaphore_signal(barrier, inc=1, device_id=(row, d), device_id_type=MESH)
-        for t in range(1, 3):
-            for d in range(1, SIDE):
-                pl.semaphore_signal(barrier, inc=1, device_id=(x_peer(d), t), device_id_type=MESH)
-
-    @pl.when(z > 0)
-    def _():
-        pl.semaphore_signal(barrier, inc=1, device_id=(row, 0), device_id_type=MESH)
-
-    @pl.when((z == 1) | (z == 2))
-    def _():
-        for d in range(1, SIDE):
-            pl.semaphore_signal(barrier, inc=1, device_id=(x_peer(d), 0), device_id_type=MESH)
-
-    partners = CHIPS + jnp.where(z == 0, 7 + 6, jnp.where(z <= 2, 1 + 3, 1))
+    signal(barrier, sib)
+    partners = CHIPS + jnp.where(z == 0, 2 * 7, jnp.where(z <= 2, 7, 1))
 
     def product(a, slot, columns):
         total = None
@@ -111,17 +112,21 @@
     def block_columns(i):
         return pl.ds(pl.multiple_of(lax.rem(x + i, SIDE) * 256, 256), 256)
 
+    def nth(t):
+        return lax.rem(t + 2, SIDE)
+
     def c_copy(a, i):
         return remote(csend.at[a, i], crecv.at[a, i], c_ssem.at[a, i], c_rsem.at[a, i], sib)
 
     def other_block(a, i):
-        csend[a, i] = product(a, 0, block_columns(i)).astype(BF16)
-
-    def own_block(a, i):
+        csend[a, i] = product(a, 0, block_columns(nth(i))).astype(BF16)
+
+    def own_block(a, turn):
+        i = nth(turn)
         columns = block_columns(i)
         total = product(a, 1, columns)
-        c_copy(a, i).wait_recv()
-        acc[...] = total + crecv[a, i].astype(F32)
+        c_copy(a, turn).wait_recv()
+        acc[...] = total + crecv[a, turn].astype(F32)
         mine = pl.ds(pl.multiple_of(16 * p, 16), 16)
         acc[mine, :] = acc[mine, :] - statv[:, a, columns]
         for t in range(2):
@@ -141,7 +146,7 @@
                 (2 * (px * SIDE + py) + c, z),
             ).start()
 
-        for j in range(SIDE):
+        for j in (2, 1, 3, 0):
             if j == 0:
                 pl.when(i > 0)(lambda: send(0))
             else:
@@ -170,75 +175,98 @@
     pl.semaphore_wait(barrier, partners)
     c_copy(0, 0).start()
 
-    def near(part, device):
-        remote(lc.at[part], lg.at[pl.ds(3 * part, 3), x, y], l_ssem.at[part], l_rsem.at[part], device).start()
+    pl.when(z > 2)(lambda: signal(ready_sem, (row, 0)))
+
+    halves = (pl.ds(0, 256), pl.ds(256, 256))
+
+    def along(h, d):
+        return y_peer(d) if h else x_peer(d)
+
+    def near(part, count):
+        for d in (2, 1, 3):
+            for h in range(2):
+                remote(
+                    lc.at[part, pl.ds(0, count), :, halves[h]],
+                    lg.at[pl.ds(3 * part, count), x, y, :, halves[h]],
+                    l_ssem.at[part, h],
+                    l_rsem.at[part, h],
+                    (along(h, d), z),
+                ).start()
 
     own_part = [pltpu.make_async_copy(lc.at[t], lg.at[pl.ds(3 * t, 3), x, y], own_sem.at[t]) for t in range(2)]
 
-    def chain_block(t, d):
-        span = pl.ds(t - 1, t)
+    def chain_near(t, h, d):
         return remote(
-            lc.at[0, pl.ds(0, t)], lg.at[span, x, y], ch_ssem.at[d], l_rsem.at[0], (x_peer(d), 0)
+            lc.at[0, pl.ds(0, t), :, halves[h]],
+            lg.at[pl.ds(t - 1, t), x, y, :, halves[h]],
+            ch_ssem.at[h, d],
+            ch_rsem.at[t - 1, h],
+            (along(h, d), 0),
         )
 
-    @pl.when(z != 0)
-    def _():
-        for d in range(1, SIDE):
-            near(0, (x_peer(d), z))
-        own_part[0].start()
-
     for t in (1, 2):
 
         @pl.when(z == t)
         def _():
             for d in range(SIDE):
-                chain_block(t, d).start()
-
-    for d in range(1, SIDE):
-        near(1, (y_peer(d), z))
+                for h in range(2):
+                    chain_near(t, h, d).start()
+            near(0, t)
+
+    pl.when(z > 2)(lambda: near(0, 3))
+    pl.when(z > 0)(lambda: own_part[0].start())
+    near(1, 3)
     own_part[1].start()
 
     stat_load.wait()
     both_halves(0, 1)
 
-    def far_source(part):
-        return lg.at[pl.ds(0, 3), :, y] if part == 0 else lg.at[pl.ds(3, 3), x]
-
-    def far(part):
-        for d in range(1, SIDE):
-            device = (y_peer(d) if part == 0 else x_peer(d), z)
-            remote(far_source(part), far_source(part), f_ssem.at[part], f_rsem.at[part], device).start()
-
-    def three_near(part):
-        return lg.at[pl.ds(3 * part, 3), 0, pl.ds(0, 3)]
-
-    def three_far(part):
-        return lg.at[pl.ds(3 * part, 3), pl.ds(0, 3)]
-
-    def near_wait(part):
-        wait_bytes(three_near(part), l_rsem.at[part])
+    def source(first, count, h):
+        span = pl.ds(first, count)
+        return lg.at[span, x, :, :, halves[h]] if h else lg.at[span, :, y, :, halves[h]]
+
+    def far(first, count, sem):
+        for h in range(2):
+            for d in (2, 1, 3):
+                device = (along(1 - h, d), z)
+                remote(
+                    source(first, count, h), source(first, count, h), f_ssem.at[sem, h], f_rsem.at[sem, h], device
+                ).start()
+
+    def three_near(first, count, h):
+        return lg.at[pl.ds(first, count), 0, pl.ds(0, 3), :, halves[h]]
+
+    def three_far(first, count, h):
+        return lg.at[pl.ds(first, count), pl.ds(0, 3), :, :, halves[h]]
+
+    def relay_chain(t):
+        for h in range(2):
+            wait_bytes(source(t - 1, t, h), ch_rsem.at[t - 1, h])
+        far(t - 1, t, 2 * t - 2)
+
+    def relay(part, count):
         own_part[part].wait()
-
-    def gather_wait(part):
-        wait_bytes(three_far(part), f_rsem.at[part])
-
-    def relay():
-        @pl.when(z != 0)
-        def _():
-            near_wait(0)
-            far(0)
-
-        near_wait(1)
-        far(1)
+        for h in range(2):
+            wait_bytes(three_near(3 * part, count, h), l_rsem.at[part, h])
+        far(3 * part, count, part)
+
+    def gather_wait(first, count, sem):
+        for h in range(2):
+            wait_bytes(three_far(first, count, h), f_rsem.at[sem, h])
+
+    @pl.when(z == 0)
+    def _():
+        relay_chain(1)
+        relay_chain(2)
+
+    def between():
+        @pl.when(z > 2)
+        def _():
+            relay(0, 3)
+            relay(1, 3)
 
     loads[2].wait()
-    both_halves(1, 0, relay)
-
-    @pl.when(z == 0)
-    def _():
-        wait_bytes(far_source(0), l_rsem.at[0])
-        far(0)
-
+    both_halves(1, 0, between)
     inv_load.wait()
 
     def reduced(a):
@@ -252,8 +280,14 @@
 
     rz[2] = red[0]
     rz_copies = [remote(rz.at[2], rz.at[t], rz_ssem, rz_rsem.at[t], (row, 0)) for t in range(2)]
-    for t in range(2):
-        pl.when(z == t + 1)(lambda: rz_copies[t].start())
+    for t in (1, 2):
+
+        @pl.when(z == t)
+        def _():
+            rz_copies[t - 1].start()
+            relay(0, t)
+            relay(1, 3)
+
 
     def applied(block, k):
         panel = lg[block].reshape(256, 512)
@@ -300,24 +334,31 @@
             if k == 0:
                 pivotal = red[0]
             elif k == 1:
-                gather_wait(0)
+                gather_wait(0, 1, 0)
                 pivotal = -applied(0, 0)
                 rz_copies[0].wait_recv()
                 pivotal = rz[0] + pivotal
             else:
+                gather_wait(1, 2, 2)
                 pivotal = -applied(1, 0) - applied(2, 1)
                 rz_copies[1].wait_recv()
                 pivotal = rz[1] + pivotal
             q[k, :, c] = pivotal.astype(BF16).reshape(8, 16, 128)
             sib_copy(k).start()
+            if k == 0:
+                pl.semaphore_wait(ready_sem, PLANES - 3)
             for d in range(1, PLANES):
                 z_copy(k, d).start()
+            if k == 0:
+                relay(1, 3)
 
         @pl.when(z != 0)
         def _():
             if k == 1:
-                gather_wait(0)
-                gather_wait(1)
+                for t in (1, 2):
+                    pl.when(z == t)(lambda: gather_wait(0, t, 0))
+                pl.when(z > 2)(lambda: gather_wait(0, 3, 0))
+                gather_wait(3, 3, 1)
                 reduced(1)
             if k > 0:
                 x_send(k - 1)
@@ -335,8 +376,8 @@
 
     @pl.when(z == 0)
     def _():
-        gather_wait(1)
         reduced(1)
+        gather_wait(3, 3, 1)
         for k in range(2):
             x_send(k)
             update(k)
@@ -385,20 +426,37 @@
         for i in range(SIDE):
             c_copy(a, i).wait_send()
         wait_bytes(rssend.at[a, pl.ds(0, CHIPS - 1)], rs_ssem.at[a])
-        wait_bytes(three_far(a), f_ssem.at[a])
-
-    @pl.when(z != 0)
-    def _():
-        wait_bytes(three_near(0), l_ssem.at[0])
-
-    wait_bytes(three_near(1), l_ssem.at[1])
+
+    def far_sent(first, count, sem):
+        for h in range(2):
+            wait_bytes(three_far(first, count, h), f_ssem.at[sem, h])
+
+    def near_sent(part, count):
+        for h in range(2):
+            wait_bytes(three_near(3 * part, count, h), l_ssem.at[part, h])
+
     for t in (1, 2):
 
         @pl.when(z == t)
         def _():
+            near_sent(0, t)
+            far_sent(0, t, 0)
             for d in range(SIDE):
-                chain_block(t, d).wait_send()
-
+                for h in range(2):
+                    chain_near(t, h, d).wait_send()
+
+    @pl.when(z > 2)
+    def _():
+        near_sent(0, 3)
+        far_sent(0, 3, 0)
+
+    @pl.when(z == 0)
+    def _():
+        far_sent(0, 1, 0)
+        far_sent(1, 2, 2)
+
+    near_sent(1, 3)
+    far_sent(3, 3, 1)
     for k in range(3):
         sib_copy(k).wait_send()
         wait_bytes(xg.at[k, pl.ds(0, CHIPS - 1)], x_ssem.at[k])
@@ -445,9 +503,10 @@
             dma((2,)),
             dma((2, 4)), dma((2, 4)),
             dma((2,)), dma((2,)),
-            dma((2,)), dma((2,)),
-            dma((2,)), dma((2,)),
-            dma((4,)),
+            dma((2, 2)), dma((2, 2)),
+            dma((3, 2)), dma((3, 2)),
+            dma((2, 4)), dma((2, 2)),
+            pltpu.SemaphoreType.REGULAR,
             dma, dma((2,)),
             dma((3, 7)), dma((3,)),
             dma((3,)), dma((3,)),

time: 51.1 us -> 47.2 us (0.924)
  the two profiles are of different devices: /device:TPU:97 before, /device:TPU:160 now
where the time goes in v3:
time: 47.2 us; the launch traced here: 47.1 us
  Pallas kernels  43.2 us (92%)
  local copies, waits for them, and re-layouts  3.2 us (7%)
  between operations  0.64 us (1%)
    pallas_call x1, Pallas kernels, per_device(): pl.pallas_call(kernel, out_shape=(jax.ShapeDtypeStruct((2, 16, 1024), F32...  43.2 us
    unnamed x2, local copies, waits for them, and re-layouts  3.2 us

profile of v3, /device:TPU:160, one launch (start us, length us, event | category | flops | bytes accessed | tf_op | source)
XLA Modules:
  0.0 47.1 jit_solution(11005700767175546454)
XLA Ops:
  0.6 43.2 %shard_map.68 = (f32[2,16,1024]{2,1,0:T(8,128)}, bf16[3,16,1024]{2,1,0:T(8,128)(2,1)}) custom-call(bf16[2,3,16,2,16,512]{5,4,3,2,1,0:T(8,128)(2,1)} %bitcast.3, bf16[3,512,1024]{2,1,0:T(8,128)(2,1)} %s.1, bf16[2,3,16,512]{3,2,1,0:T(8,128)(2,1)} %lc.1, bf16[3,512,512]{2,1,0:T(8,128)(2,1)} %inv.1, f32[16,2,1024]{2,1,0:T(2,128)} %stat.1), custom_call_target="tpu_custom_call" | custom-call | flops 3400000000 | bytes 9000000 | tf_op jit(solution)/shard_map/pallas_call | solution.py:476
  43.9 1.7 %copy.7 = f32[16,2,1024]{2,1,0:T(2,128)} copy(f32[16,2,1024]{2,0,1:T(8,128)} %bitcast.2) | data formatting | bytes 262144
  45.6 1.5 %copy.9 = bf16[3,16,1024]{2,1,0:T(8,128)(2,1)} copy(bf16[3,16,1024]{2,1,0:T(8,128)(2,1)} %get-tuple-element.11) | data formatting | bytes 196608

commit v4 on v3

v4 whole, which is shorter than its diff:
```python
import jax
import jax.numpy as jnp
from jax import lax
from jax.experimental import pallas as pl
from jax.experimental.pallas import tpu as pltpu
from jax.sharding import PartitionSpec as P

MESH = pl.DeviceIdType.MESH
F32 = jnp.float32
BF16 = jnp.bfloat16
SIDE = 4
CHIPS = 16
PLANES = 8


def lanes_low(shape):
    return lax.broadcasted_iota(jnp.int32, shape, len(shape) - 1) < 64


def swap(value):
    return pltpu.roll(value, 64, 1)


def dot(a, b):
    return jnp.dot(a, b, preferred_element_type=F32)


def wait_bytes(ref, sem):
    pltpu.make_async_copy(ref, ref, sem).wait()


def kernel(
    le, s, lc, inv, stat, ug, xg,
    sv, lev, invv, statv, csend, crecv, acc, rssend, rsrecv, mid, last, lg, rz, q, xs, usend, red,
    le_sem, load_sem, mine_sem, own_sem, c_ssem, c_rsem, rs_ssem, rs_rsem, l_ssem, l_rsem, f_ssem, f_rsem, ch_ssem, ch_rsem, ready_sem,
    r2_ssem, r2_rsem, rz_ssem, rz_rsem, z_ssem, z_rsem, q_ssem, q_rsem, x_ssem, x_rsem, u_ssem, u_rsem,
):
    row = lax.axis_index("row")
    z = lax.axis_index("col")
    c = lax.rem(row, 2)
    p = row // 2
    x = p // SIDE
    y = lax.rem(p, SIDE)
    sib = (row + 1 - 2 * c, z)
    low = lanes_low((128, 128))
    steps = (0, 1, 2, 1)
    by_distance = sorted(range(1, CHIPS), key=lambda d: -steps[d // SIDE] - steps[d % SIDE])

    def peer(d):
        px = lax.rem(x + d // SIDE, SIDE)
        py = lax.rem(y + lax.rem(d, SIDE), SIDE)
        return px * SIDE + py

    def x_peer(d):
        return 2 * (lax.rem(x + d, SIDE) * SIDE + y) + c

    def y_peer(d):
        return 2 * (x * SIDE + lax.rem(y + d, SIDE)) + c

    def remote(src, dst, ssem, rsem, device):
        return pltpu.make_async_remote_copy(
            src_ref=src, dst_ref=dst, send_sem=ssem, recv_sem=rsem, device_id=device, device_id_type=MESH
        )

    def block_columns(i):
        return pl.ds(pl.multiple_of(lax.rem(x + i, SIDE) * 256, 256), 256)

    def nth(t):
        return lax.rem(t + 2, SIDE)

    def le_load(a, slot, b):
        half = c if slot else 1 - c
        return pltpu.make_async_copy(
            le.at[a, b, :, half], lev.at[a, slot, :, :, pl.ds(512 * b, 512)], le_sem.at[a, slot, b]
        )

    def s_load(t):
        columns = block_columns(nth(t))
        return pltpu.make_async_copy(s.at[:, columns], sv.at[:, columns], load_sem.at[t])

    def le_loads(a):
        return [le_load(a, slot, b) for slot in range(2) for b in range(3)]

    inv_load = pltpu.make_async_copy(inv, invv, load_sem.at[4])
    stat_load = pltpu.make_async_copy(stat, statv, load_sem.at[5])
    for cp in le_loads(0) + [s_load(t) for t in range(SIDE)] + le_loads(1) + [stat_load, inv_load]:
        cp.start()

    barrier = pltpu.get_barrier_semaphore()

    def greet(d, carry):
        pl.semaphore_signal(barrier, inc=1, device_id=(2 * peer(d) + c, z), device_id_type=MESH)
        return carry

    def signal(sem, device):
        pl.semaphore_signal(sem, inc=1, device_id=device, device_id_type=MESH)

    @pl.when(z == 0)
    def _():
        for d in (4, 3, 5, 6, 7, 2, 1):
            signal(barrier, (row, d))
        for t in (2, 1):
            for d in (2, 1, 3):
                signal(barrier, (x_peer(d), t))
                signal(barrier, (y_peer(d), t))

    @pl.when((z == 1) | (z == 2))
    def _():
        signal(barrier, (row, 0))
        for d in (2, 1, 3):
            signal(barrier, (x_peer(d), 0))
            signal(barrier, (y_peer(d), 0))

    lax.fori_loop(1, CHIPS, greet, 0)
    signal(barrier, sib)
    partners = CHIPS + jnp.where(z == 0, 2 * 7, jnp.where(z <= 2, 7, 1))

    def c_copy(a, i):
        return remote(csend.at[a, i], crecv.at[a, i], c_ssem.at[a, i], c_rsem.at[a, i], sib)

    def multiply(a, t):
        if a == 0:
            s_load(t).wait()
        both = dot(lev[a].reshape(512, 1536), sv[:, block_columns(nth(t))])
        csend[a, t] = both[0:256].astype(BF16)
        acc[t] = both[256:512]

    def rs_send(a, i, j):
        py = lax.rem(y + j, SIDE)
        px = lax.rem(x + i, SIDE)
        remote(
            rssend.at[a, i, py],
            rsrecv.at[SIDE * i + j],
            rs_ssem.at[a, 0],
            rs_rsem.at[a, 0],
            (2 * (px * SIDE + py) + c, z),
        ).start()

    top, bottom = pl.ds(0, 64), pl.ds(64, 64)

    def first_x(a, i):
        remote(
            rssend.at[a, i, :, top],
            mid.at[a, 0, i],
            rs_ssem.at[a, 0],
            rs_rsem.at[a, 0],
            (2 * (lax.rem(x + i, SIDE) * SIDE + y) + c, z),
        ).start()

    def first_y(a):
        for j in (2, 1, 3):
            remote(
                rssend.at[a, :, lax.rem(y + j, SIDE), bottom],
                mid.at[a, 1, j],
                rs_ssem.at[a, 1],
                rs_rsem.at[a, 1],
                (y_peer(j), z),
            ).start()

    def rs_relay(a):
        wait_bytes(mid.at[a, 0, pl.ds(1, 3)], rs_rsem.at[a, 0])
        total = rssend[a, 0, :, 0:64].astype(F32)
        for d in range(1, SIDE):
            total = total + mid[a, 0, d].astype(F32)
        mid[a, 0, 0] = total.astype(BF16)
        for j in (2, 1, 3):
            remote(
                mid.at[a, 0, 0, lax.rem(y + j, SIDE)], last.at[a, 0, j], r2_ssem.at[a, 0], r2_rsem.at[a, 0], (y_peer(j), z)
            ).start()
        wait_bytes(mid.at[a, 1, pl.ds(1, 3)], rs_rsem.at[a, 1])
        total = rssend[a, :, y, 64:128].astype(F32)
        for d in range(1, SIDE):
            total = total + mid[a, 1, d].astype(F32)
        mid[a, 1, 0] = total.astype(BF16)
        for i in (2, 1, 3):
            remote(
                mid.at[a, 1, 0, i], last.at[a, 1, i], r2_ssem.at[a, 1], r2_rsem.at[a, 1], (x_peer(i), z)
            ).start()

    def rs_last(a):
        for h in range(2):
            wait_bytes(last.at[a, h, pl.ds(1, 3)], r2_rsem.at[a, h])
            total = mid[a, h, 0, (0 if h else y)].astype(F32)
            for d in range(1, SIDE):
                total = total + last[a, h, d].astype(F32)
            red[a, 64 * h : 64 * h + 64] = -total

    def rs_sent(a):
        for h in range(2):
            wait_bytes(mid.at[a, h, pl.ds(1, 3)], rs_ssem.at[a, h])
            wait_bytes(last.at[a, h, pl.ds(1, 3)], r2_ssem.at[a, h])

    def finish(a, turn):
        i = nth(turn)
        columns = block_columns(i)
        c_copy(a, turn).wait_recv()
        acc[turn] = acc[turn] + crecv[a, turn].astype(F32)
        mine = pl.ds(pl.multiple_of(16 * p, 16), 16)
        acc[turn, mine, :] = acc[turn, mine, :] - statv[:, a, columns]
        for t in range(2):
            lo = acc[turn, 0:128, 128 * t : 128 * t + 128]
            hi = acc[turn, 128:256, 128 * t : 128 * t + 128]
            rssend[a, i, 2 * t] = jnp.where(low, lo, swap(hi)).astype(BF16)
            rssend[a, i, 2 * t + 1] = jnp.where(low, swap(lo), hi).astype(BF16)

        def sends():
            for j in (2, 1, 3):
                rs_send(a, i, j)
            pl.when(i > 0)(lambda: rs_send(a, i, 0))

        if a == 0:
            pl.when(z <= 2)(sends)
            pl.when((z > 2) & (i > 0))(lambda: first_x(a, i))
        else:
            pl.when(i > 0)(lambda: first_x(a, i))

    def turns(a, first, last_turn):
        def turn(t, carry):
            @pl.when(t < SIDE)
            def _():
                multiply(a, t)
                c_copy(a, t).start()

            pl.when(t >= 2)(lambda: finish(a, t - 2))
            return carry

        lax.fori_loop(first, last_turn, turn, 0)

    for cp in le_loads(0):
        cp.wait()
    multiply(0, 0)
    pl.semaphore_wait(barrier, partners)
    c_copy(0, 0).start()

    pl.when(z > 2)(lambda: signal(ready_sem, (row, 0)))

    halves = (pl.ds(0, 256), pl.ds(256, 256))

    def along(h, d):
        return y_peer(d) if h else x_peer(d)

    def own_slot(part, h, span):
        return lg.at[part, 1, x, y, span] if h else lg.at[part, 0, y, x, span]

    def near(part, count):
        for d in (2, 1, 3):
            for h in range(2):
                remote(
                    lc.at[part, pl.ds(0, count), :, halves[h]],
                    own_slot(part, h, pl.ds(0, count)),
                    l_ssem.at[part, h],
                    l_rsem.at[part, h],
                    (along(h, d), z),
                ).start()

    own_part = [
        [
            pltpu.make_async_copy(lc.at[t, :, :, halves[h]], own_slot(t, h, pl.ds(0, 3)), own_sem.at[t, h])
            for h in range(2)
        ]
        for t in range(2)
    ]

    def own_start(part):
        for cp in own_part[part]:
            cp.start()

    def chain_near(t, h, d):
        return remote(
            lc.at[0, pl.ds(0, t), :, halves[h]],
            own_slot(0, h, pl.ds(t - 1, t)),
            ch_ssem.at[h, d],
            ch_rsem.at[t - 1, h],
            (along(h, d), 0),
        )

    for t in (1, 2):

        @pl.when(z == t)
        def _():
            for d in range(SIDE):
                for h in range(2):
                    chain_near(t, h, d).start()
            near(0, t)

    pl.when(z > 2)(lambda: near(0, 3))
    pl.when(z > 0)(lambda: own_start(0))
    near(1, 3)
    own_start(1)

    stat_load.wait()
    turns(0, 1, SIDE + 2)
    pl.when(z > 2)(lambda: first_y(0))

    def source(part, span, h):
        return lg.at[part, 1, x, :, span] if h else lg.at[part, 0, y, :, span]

    def far(part, span, sem):
        for h in range(2):
            for d in (2, 1, 3):
                device = (along(1 - h, d), z)
                remote(
                    source(part, span, h), source(part, span, h), f_ssem.at[sem, h], f_rsem.at[sem, h], device
                ).start()

    def three_near(part, span, h):
        return lg.at[part, h, 0, pl.ds(0, 3), span]

    def three_far(part, span, h):
        return lg.at[part, h, pl.ds(0, 3), :, span]

    def relay_chain(t):
        for h in range(2):
            wait_bytes(source(0, pl.ds(t - 1, t), h), ch_rsem.at[t - 1, h])
        far(0, pl.ds(t - 1, t), 2 * t - 2)

    def relay(part, count):
        for cp in own_part[part]:
            cp.wait()
        for h in range(2):
            wait_bytes(three_near(part, pl.ds(0, count), h), l_rsem.at[part, h])
        far(part, pl.ds(0, count), part)

    def gather_wait(part, span, sem):
        for h in range(2):
            wait_bytes(three_far(part, span, h), f_rsem.at[sem, h])

    @pl.when(z == 0)
    def _():
        relay_chain(1)
        relay_chain(2)

    def between():
        @pl.when(z > 2)
        def _():
            relay(0, 3)
            relay(1, 3)

    for cp in le_loads(1):
        cp.wait()
    turns(1, 0, 3)
    between()
    turns(1, 3, SIDE + 2)
    first_y(1)
    inv_load.wait()

    @pl.when(z <= 2)
    def _():
        wait_bytes(rsrecv.at[pl.ds(1, CHIPS - 1)], rs_rsem.at[0, 0])
        total = rssend[0, 0, y].astype(F32)
        for d in range(1, CHIPS):
            total = total + rsrecv[d].astype(F32)
        red[0] = -total

    @pl.when(z > 2)
    def _():
        rs_relay(0)
        rs_relay(1)
        rs_last(0)

    rz[2] = red[0]
    rz_copies = [remote(rz.at[2], rz.at[t], rz_ssem, rz_rsem.at[t], (row, 0)) for t in range(2)]
    for t in (1, 2):

        @pl.when(z == t)
        def _():
            rz_copies[t - 1].start()
            relay(0, t)
            relay(1, 3)
            rs_relay(1)


    def applied(block, k):
        part, slot = divmod(block, 3)
        solved = xs[k].reshape(256, 128)
        chips = [(i, j) for i in range(SIDE) for j in range(SIDE)]
        first = dot(jnp.concatenate([lg[part, 0, j, i, slot] for i, j in chips], axis=0), solved)
        second = dot(jnp.concatenate([lg[part, 1, i, j, slot] for i, j in chips], axis=0), solved)
        return jnp.where(low, first[0:128], second[128:256]) + swap(
            jnp.where(low, first[128:256], second[0:128])
        )

    def update(k):
        red[1] = red[1] - applied(3 + k, k)

        @pl.when(z > k)
        def _():
            red[0] = red[0] - applied(k, k)

    def own_x(k):
        return pltpu.make_async_copy(xs.at[k, lax.rem(p, 8), c], xg.at[k, p], mine_sem.at[k])

    def x_send(k):
        def send(d, carry):
            target = peer(d)
            remote(
                xs.at[k, lax.rem(target, 8), c], xg.at[k, p], x_ssem.at[k], x_rsem.at[k], (2 * target + c, z)
            ).start()
            return carry

        lax.fori_loop(1, CHIPS, send, 0)
        own_x(k).start()

    def z_copy(k, d):
        return remote(
            q.at[k, c], q.at[k, c], z_ssem.at[k, d - 1], z_rsem.at[k], (row, lax.rem(z + d, PLANES))
        )

    def sib_copy(k):
        return remote(q.at[k, c], q.at[k, c], q_ssem.at[k], q_rsem.at[k], sib)

    def sib_back(k):
        return remote(q.at[k, 1 - c], q.at[k, 1 - c], q_ssem.at[k], q_rsem.at[k], sib)

    for k in range(3):

        @pl.when(z == 0)
        def _():
            if k == 0:
                pivotal = red[0]
            elif k == 1:
                gather_wait(0, pl.ds(0, 1), 0)
                pivotal = -applied(0, 0)
                rz_copies[0].wait_recv()
                pivotal = rz[0] + pivotal
            else:
                gather_wait(0, pl.ds(1, 2), 2)
                pivotal = -applied(1, 0) - applied(2, 1)
                rz_copies[1].wait_recv()
                pivotal = rz[1] + pivotal
            q[k, c] = pivotal.astype(BF16).reshape(8, 16, 128)
            sib_copy(k).start()
            if k == 0:
                pl.semaphore_wait(ready_sem, PLANES - 3)
            for d in (4, 5, 3, 6, 2, 7, 1):
                z_copy(k, d).start()
            if k == 0:
                relay(1, 3)
                rs_relay(1)

        @pl.when(z != 0)
        def _():
            if k == 1:
                for t in (1, 2):
                    pl.when(z == t)(lambda: gather_wait(0, pl.ds(0, t), 0))
                pl.when(z > 2)(lambda: gather_wait(0, pl.ds(0, 3), 0))
                gather_wait(1, pl.ds(0, 3), 1)
                rs_last(1)
            if k > 0:
                x_send(k - 1)
                update(k - 1)
            z_copy(k, 1).wait_recv()
            sib_copy(k).start()

        sib_back(k).wait_recv()
        pivotal = jnp.concatenate([q[k, h, g] for g in range(8) for h in range(2)], axis=0)
        left = dot(invv[k, :, 0:256], pivotal)
        right = dot(invv[k, 256:512, 256:512], pivotal)
        low_x = lanes_low((256, 128))
        solved = jnp.where(low_x, left[0:256], right + swap(left[256:512]))
        xs[k] = solved.astype(BF16).reshape(8, 2, 16, 128)

    @pl.when(z == 0)
    def _():
        rs_last(1)
        gather_wait(1, pl.ds(0, 3), 1)
        for k in range(2):
            x_send(k)
            update(k)

    @pl.when((z == 1) | (z == 2))
    def _():
        wait_bytes(rz.at[2], rz_ssem)

    update(2)
    first, second = red[0], red[1]
    usend[0:8, 0:16] = jnp.where(low, first, swap(second)).astype(BF16).reshape(8, 16, 128)
    usend[8:16, 0:16] = jnp.where(low, swap(first), second).astype(BF16).reshape(8, 16, 128)
    for t in range(CHIPS):
        usend[t, 16:32] = xs[2, t % 8, c]
    for d in by_distance:
        target = peer(d)
        remote(usend.at[target], ug.at[p], u_ssem, u_rsem, (2 * target + c, z)).start()
    own_u = pltpu.make_async_copy(usend.at[p], ug.at[p], mine_sem.at[2])
    own_u.start()

    for a in range(2):
        for i in range(SIDE):
            c_copy(a, i).wait_send()

    def far_sent(part, span, sem):
        for h in range(2):
            wait_bytes(three_far(part, span, h), f_ssem.at[sem, h])

    def near_sent(part, count):
        for h in range(2):
            wait_bytes(three_near(part, pl.ds(0, count), h), l_ssem.at[part, h])

    for t in (1, 2):

        @pl.when(z == t)
        def _():
            near_sent(0, t)
            far_sent(0, pl.ds(0, t), 0)
            for d in range(SIDE):
                for h in range(2):
                    chain_near(t, h, d).wait_send()

    @pl.when(z > 2)
    def _():
        near_sent(0, 3)
        far_sent(0, pl.ds(0, 3), 0)

    @pl.when(z == 0)
    def _():
        far_sent(0, pl.ds(0, 1), 0)
        far_sent(0, pl.ds(1, 2), 2)

    near_sent(1, 3)
    far_sent(1, pl.ds(0, 3), 1)
    pl.when(z <= 2)(lambda: wait_bytes(rsrecv.at[pl.ds(1, CHIPS - 1)], rs_ssem.at[0, 0]))
    pl.when(z > 2)(lambda: rs_sent(0))
    rs_sent(1)
    for k in range(3):
        sib_copy(k).wait_send()
        if k < 2:
            wait_bytes(xg.at[k, pl.ds(0, CHIPS - 1)], x_ssem.at[k])
            wait_bytes(xg.at[k, pl.ds(0, CHIPS - 1)], x_rsem.at[k])
            own_x(k).wait()

        @pl.when(z == 0)
        def _():
            for d in range(1, PLANES):
                z_copy(k, d).wait_send()

    wait_bytes(ug.at[pl.ds(0, CHIPS - 1)], u_ssem)
    own_u.wait()
    wait_bytes(ug.at[pl.ds(0, CHIPS - 1)], u_rsem)


def assemble(ug, xg, upd, sol):
    low = lanes_low((16, 128))
    early = lax.axis_index("row") < CHIPS
    for t in range(8):
        columns = slice(128 * t, 128 * t + 128)
        even, odd = ug[2 * t, 0:16].astype(F32), ug[2 * t + 1, 0:16].astype(F32)
        upd[:, 0, columns] = jnp.where(low, even, swap(odd))
        upd[:, 1, columns] = jnp.where(low, swap(even), odd)
        for k in range(3):
            even = ug[2 * t, 16:32] if k == 2 else xg[k, 2 * t]
            odd = ug[2 * t + 1, 16:32] if k == 2 else xg[k, 2 * t + 1]
            even, odd = even.astype(F32), odd.astype(F32)
            value = jnp.where(early, jnp.where(low, even, swap(odd)), jnp.where(low, swap(even), odd))
            sol[k, :, columns] = value.astype(BF16)


def per_device(lower_earlier, lower_current, inverse_diagonal, solved_earlier, statistics):
    dma = pltpu.SemaphoreType.DMA
    any_space = pl.BlockSpec(memory_space=pl.ANY)
    vmem = pl.BlockSpec(memory_space=pltpu.VMEM)
    pieces, solved = pl.pallas_call(
        kernel,
        out_shape=(
            jax.ShapeDtypeStruct((16, 32, 128), BF16),
            jax.ShapeDtypeStruct((2, 16, 16, 128), BF16),
        ),
        in_specs=[any_space] * 5,
        out_specs=(any_space, any_space),
        scratch_shapes=[
            pltpu.VMEM((1536, 1024), BF16),
            pltpu.VMEM((2, 2, 16, 16, 1536), BF16),
            pltpu.VMEM((3, 512, 512), BF16),
            pltpu.VMEM((16, 2, 1024), F32),
            pltpu.VMEM((2, 4, 256, 256), BF16),
            pltpu.VMEM((2, 4, 256, 256), BF16),
            pltpu.VMEM((4, 256, 256), F32),
            pltpu.VMEM((2, 4, 4, 128, 128), BF16),
            pltpu.VMEM((16, 128, 128), BF16),
            pltpu.VMEM((2, 2, 4, 4, 64, 128), BF16),
            pltpu.VMEM((2, 2, 4, 64, 128), BF16),
            pltpu.VMEM((2, 2, 4, 4, 3, 16, 256), BF16),
            pltpu.VMEM((3, 128, 128), F32),
            pltpu.VMEM((3, 2, 8, 16, 128), BF16),
            pltpu.VMEM((3, 8, 2, 16, 128), BF16),
            pltpu.VMEM((16, 32, 128), BF16),
            pltpu.VMEM((2, 128, 128), F32),
            dma((2, 2, 3)),
            dma((6,)),
            dma((3,)),
            dma((2, 2)),
            dma((2, 4)), dma((2, 4)),
            dma((2, 2)), dma((2, 2)),
            dma((2, 2)), dma((2, 2)),
            dma((3, 2)), dma((3, 2)),
            dma((2, 4)), dma((2, 2)),
            pltpu.SemaphoreType.REGULAR,
            dma((2, 2)), dma((2, 2)),
            dma, dma((2,)),
            dma((3, 7)), dma((3,)),
            dma((3,)), dma((3,)),
            dma((2,)), dma((2,)),
            dma, dma,
        ],
        compiler_params=pltpu.CompilerParams(
            collective_id=0, has_side_effects=True, vmem_limit_bytes=56 * 1024 * 1024
        ),
        cost_estimate=pl.CostEstimate(flops=3400000000, bytes_accessed=9000000, transcendentals=0),
    )(
        lower_earlier.reshape(2, 3, 16, 2, 16, 512),
        solved_earlier.reshape(1536, 1024),
        lower_current,
        inverse_diagonal,
        statistics,
    )
    return pl.pallas_call(
        assemble,
        out_shape=(
            jax.ShapeDtypeStruct((16, 2, 1024), F32),
            jax.ShapeDtypeStruct((3, 16, 1024), BF16),
        ),
        in_specs=[vmem, vmem],
        out_specs=(vmem, vmem),
        cost_estimate=pl.CostEstimate(flops=200000, bytes_accessed=500000, transcendentals=0),
    )(pieces, solved)


def solution(mesh):
    placed = (
        P("col", "row", None, None),
        P("col", None, "row", None),
        P(),
        P("row", None, None),
        P("row", "col", None),
    )
    return jax.shard_map(
        per_device,
        mesh=mesh,
        in_specs=placed,
        out_specs=(P("row", "col", None), P(None, "row", None)),
        check_vma=False,
    )
```

time: 47.2 us -> 44.4 us (0.941)
  the two profiles are of different devices: /device:TPU:160 before, /device:TPU:32 now
where the time goes in v4:
time: 44.4 us; the launch traced here: 44.3 us
  Pallas kernels  43.7 us (98%)
  between operations  0.64 us (1%)
    pallas_call x1, Pallas kernels, per_device(): pl.pallas_call(kernel, out_shape=(jax.ShapeDtypeStruct((16, 32, 128), BF1...  41.9 us
    pallas_call x1, Pallas kernels, per_device(): pl.pallas_call(assemble, out_shape=(jax.ShapeDtypeStruct((16, 2, 1024), F...  1.83 us

profile of v4, /device:TPU:32, one launch (start us, length us, event | category | flops | bytes accessed | tf_op | source)
XLA Modules:
  0.0 44.3 jit_solution(10814439837723667758)
XLA Ops:
  0.6 41.9 %shard_map.68 = (bf16[16,32,128]{2,1,0:T(8,128)(2,1)}, bf16[2,16,16,128]{3,2,1,0:T(8,128)(2,1)}) custom-call(bf16[2,3,16,2,16,512]{5,4,3,2,1,0:T(8,128)(2,1)} %bitcast.2, bf16[1536,1024]{1,0:T(8,128)(2,1)} %bitcast.3, bf16[2,3,16,512]{3,2,1,0:T(8,128)(2,1)} %lc.1, bf16[3,512,512]{2,1,0:T(8,128)(2,1)} %inv.1, f32[16,2,1024]{2,1,0:T(2,128)} %stat.1), custom_call_target="tpu_custom_call" | custom-call | flops 3400000000 | bytes 9000000 | tf_op jit(solution)/shard_map/pallas_call | solution.py:561
  42.5 1.8 %shard_map.69 = (f32[16,2,1024]{2,1,0:T(2,128)}, bf16[3,16,1024]{2,1,0:T(8,128)(2,1)}) custom-call(bf16[16,32,128]{2,1,0:T(8,128)(2,1)} %get-tuple-element.4.ug, bf16[2,16,16,128]{3,2,1,0:T(8,128)(2,1)} %get-tuple-element.5.xg), custom_call_target="tpu_custom_call" | custom-call | flops 200000 | bytes 500000 | tf_op jit(solution)/shard_map/pallas_call | solution.py:615

commit v5 on v4

--- a/solution.py
+++ b/solution.py
@@ -31,9 +31,9 @@
 
 def kernel(
     le, s, lc, inv, stat, ug, xg,
-    sv, lev, invv, statv, csend, crecv, acc, rssend, rsrecv, mid, last, lg, rz, q, xs, usend, red,
-    le_sem, load_sem, mine_sem, own_sem, c_ssem, c_rsem, rs_ssem, rs_rsem, l_ssem, l_rsem, f_ssem, f_rsem, ch_ssem, ch_rsem, ready_sem,
-    r2_ssem, r2_rsem, rz_ssem, rz_rsem, z_ssem, z_rsem, q_ssem, q_rsem, x_ssem, x_rsem, u_ssem, u_rsem,
+    sv, lev, invv, statv, csend, crecv, acc, rssend, rsrecv, mid, last, lg, q, xs, usend, red,
+    le_sem, load_sem, mine_sem, own_sem, c_ssem, c_rsem, rs_ssem, rs_rsem, l_ssem, l_rsem, f_ssem, f_rsem, ready_sem,
+    r2_ssem, r2_rsem, z_ssem, z_rsem, q_ssem, q_rsem, x_ssem, x_rsem, u_ssem, u_rsem,
 ):
     row = lax.axis_index("row")
     z = lax.axis_index("col")
@@ -95,25 +95,14 @@
     def signal(sem, device):
         pl.semaphore_signal(sem, inc=1, device_id=device, device_id_type=MESH)
 
-    @pl.when(z == 0)
+    @pl.when(z <= 2)
     def _():
         for d in (4, 3, 5, 6, 7, 2, 1):
-            signal(barrier, (row, d))
-        for t in (2, 1):
-            for d in (2, 1, 3):
-                signal(barrier, (x_peer(d), t))
-                signal(barrier, (y_peer(d), t))
-
-    @pl.when((z == 1) | (z == 2))
-    def _():
-        signal(barrier, (row, 0))
-        for d in (2, 1, 3):
-            signal(barrier, (x_peer(d), 0))
-            signal(barrier, (y_peer(d), 0))
+            signal(barrier, (row, lax.rem(z + d, PLANES)))
 
     lax.fori_loop(1, CHIPS, greet, 0)
     signal(barrier, sib)
-    partners = CHIPS + jnp.where(z == 0, 2 * 7, jnp.where(z <= 2, 7, 1))
+    partners = CHIPS + jnp.where(z <= 2, 2, 3)
 
     def c_copy(a, i):
         return remote(csend.at[a, i], crecv.at[a, i], c_ssem.at[a, i], c_rsem.at[a, i], sib)
@@ -232,7 +221,10 @@
     pl.semaphore_wait(barrier, partners)
     c_copy(0, 0).start()
 
-    pl.when(z > 2)(lambda: signal(ready_sem, (row, 0)))
+    @pl.when(z > 2)
+    def _():
+        for t in range(3):
+            signal(ready_sem, (row, t))
 
     halves = (pl.ds(0, 256), pl.ds(256, 256))
 
@@ -265,24 +257,8 @@
         for cp in own_part[part]:
             cp.start()
 
-    def chain_near(t, h, d):
-        return remote(
-            lc.at[0, pl.ds(0, t), :, halves[h]],
-            own_slot(0, h, pl.ds(t - 1, t)),
-            ch_ssem.at[h, d],
-            ch_rsem.at[t - 1, h],
-            (along(h, d), 0),
-        )
-
     for t in (1, 2):
-
-        @pl.when(z == t)
-        def _():
-            for d in range(SIDE):
-                for h in range(2):
-                    chain_near(t, h, d).start()
-            near(0, t)
-
+        pl.when(z == t)(lambda: near(0, t))
     pl.when(z > 2)(lambda: near(0, 3))
     pl.when(z > 0)(lambda: own_start(0))
     near(1, 3)
@@ -309,11 +285,6 @@
     def three_far(part, span, h):
         return lg.at[part, h, pl.ds(0, 3), :, span]
 
-    def relay_chain(t):
-        for h in range(2):
-            wait_bytes(source(0, pl.ds(t - 1, t), h), ch_rsem.at[t - 1, h])
-        far(0, pl.ds(t - 1, t), 2 * t - 2)
-
     def relay(part, count):
         for cp in own_part[part]:
             cp.wait()
@@ -325,10 +296,8 @@
         for h in range(2):
             wait_bytes(three_far(part, span, h), f_rsem.at[sem, h])
 
-    @pl.when(z == 0)
-    def _():
-        relay_chain(1)
-        relay_chain(2)
+    for t in (1, 2):
+        pl.when(z == t)(lambda: relay(0, t))
 
     def between():
         @pl.when(z > 2)
@@ -358,17 +327,10 @@
         rs_relay(1)
         rs_last(0)
 
-    rz[2] = red[0]
-    rz_copies = [remote(rz.at[2], rz.at[t], rz_ssem, rz_rsem.at[t], (row, 0)) for t in range(2)]
-    for t in (1, 2):
-
-        @pl.when(z == t)
-        def _():
-            rz_copies[t - 1].start()
-            relay(0, t)
-            relay(1, 3)
-            rs_relay(1)
-
+    @pl.when((z == 1) | (z == 2))
+    def _():
+        relay(1, 3)
+        rs_relay(1)
 
     def applied(block, k):
         part, slot = divmod(block, 3)
@@ -380,12 +342,12 @@
             jnp.where(low, first[128:256], second[0:128])
         )
 
-    def update(k):
-        red[1] = red[1] - applied(3 + k, k)
-
-        @pl.when(z > k)
-        def _():
-            red[0] = red[0] - applied(k, k)
+    def update(part, k):
+        red[part] = red[part] - applied(3 * part + k, k)
+
+    def a1_ready():
+        gather_wait(1, pl.ds(0, 3), 1)
+        rs_last(1)
 
     def own_x(k):
         return pltpu.make_async_copy(xs.at[k, lax.rem(p, 8), c], xg.at[k, p], mine_sem.at[k])
@@ -412,45 +374,43 @@
     def sib_back(k):
         return remote(q.at[k, 1 - c], q.at[k, 1 - c], q_ssem.at[k], q_rsem.at[k], sib)
 
+    orders = ((1, 2, 4, 5, 3, 6, 7), (1, 4, 5, 3, 6, 2, 7), (6, 3, 7, 2, 5, 1, 4))
     for k in range(3):
 
-        @pl.when(z == 0)
+        @pl.when(z == k)
         def _():
-            if k == 0:
-                pivotal = red[0]
-            elif k == 1:
-                gather_wait(0, pl.ds(0, 1), 0)
-                pivotal = -applied(0, 0)
-                rz_copies[0].wait_recv()
-                pivotal = rz[0] + pivotal
-            else:
-                gather_wait(0, pl.ds(1, 2), 2)
-                pivotal = -applied(1, 0) - applied(2, 1)
-                rz_copies[1].wait_recv()
-                pivotal = rz[1] + pivotal
-            q[k, c] = pivotal.astype(BF16).reshape(8, 16, 128)
+            q[k, c] = red[0].astype(BF16).reshape(8, 16, 128)
             sib_copy(k).start()
-            if k == 0:
-                pl.semaphore_wait(ready_sem, PLANES - 3)
-            for d in (4, 5, 3, 6, 2, 7, 1):
+            pl.semaphore_wait(ready_sem, PLANES - 3)
+            for d in orders[k]:
                 z_copy(k, d).start()
             if k == 0:
                 relay(1, 3)
                 rs_relay(1)
 
-        @pl.when(z != 0)
+        @pl.when(z != k)
         def _():
-            if k == 1:
-                for t in (1, 2):
-                    pl.when(z == t)(lambda: gather_wait(0, pl.ds(0, t), 0))
-                pl.when(z > 2)(lambda: gather_wait(0, pl.ds(0, 3), 0))
-                gather_wait(1, pl.ds(0, 3), 1)
-                rs_last(1)
             if k > 0:
-                x_send(k - 1)
-                update(k - 1)
+                pl.when((z == 0) | (z > 2))(lambda: x_send(k - 1))
+            if k == 2:
+
+                @pl.when(z == 1)
+                def _():
+                    x_send(0)
+                    x_send(1)
+
             z_copy(k, 1).wait_recv()
             sib_copy(k).start()
+            if k == 2:
+
+                @pl.when(z != 2)
+                def _():
+                    pl.when(z > 2)(lambda: gather_wait(0, pl.ds(0, 3), 0))
+                    a1_ready()
+                    for j in range(2):
+                        update(1, j)
+                        pl.when(z > 2)(lambda: update(0, j))
+
 
         sib_back(k).wait_recv()
         pivotal = jnp.concatenate([q[k, h, g] for g in range(8) for h in range(2)], axis=0)
@@ -460,19 +420,26 @@
         solved = jnp.where(low_x, left[0:256], right + swap(left[256:512]))
         xs[k] = solved.astype(BF16).reshape(8, 2, 16, 128)
 
-    @pl.when(z == 0)
-    def _():
-        rs_last(1)
-        gather_wait(1, pl.ds(0, 3), 1)
-        for k in range(2):
-            x_send(k)
-            update(k)
-
-    @pl.when((z == 1) | (z == 2))
-    def _():
-        wait_bytes(rz.at[2], rz_ssem)
-
-    update(2)
+        if k == 0:
+            for t in (1, 2):
+
+                @pl.when(z == t)
+                def _():
+                    gather_wait(0, pl.ds(0, t), 0)
+                    update(0, 0)
+
+        if k == 1:
+            pl.when(z == 2)(lambda: update(0, 1))
+
+    @pl.when(z == 2)
+    def _():
+        a1_ready()
+        for j in range(2):
+            x_send(j)
+            update(1, j)
+
+    update(1, 2)
+    pl.when(z > 2)(lambda: update(0, 2))
     first, second = red[0], red[1]
     usend[0:8, 0:16] = jnp.where(low, first, swap(second)).astype(BF16).reshape(8, 16, 128)
     usend[8:16, 0:16] = jnp.where(low, swap(first), second).astype(BF16).reshape(8, 16, 128)
@@ -502,19 +469,11 @@
         def _():
             near_sent(0, t)
             far_sent(0, pl.ds(0, t), 0)
-            for d in range(SIDE):
-                for h in range(2):
-                    chain_near(t, h, d).wait_send()
 
     @pl.when(z > 2)
     def _():
         near_sent(0, 3)
         far_sent(0, pl.ds(0, 3), 0)
-
-    @pl.when(z == 0)
-    def _():
-        far_sent(0, pl.ds(0, 1), 0)
-        far_sent(0, pl.ds(1, 2), 2)
 
     near_sent(1, 3)
     far_sent(1, pl.ds(0, 3), 1)
@@ -528,7 +487,7 @@
             wait_bytes(xg.at[k, pl.ds(0, CHIPS - 1)], x_rsem.at[k])
             own_x(k).wait()
 
-        @pl.when(z == 0)
+        @pl.when(z == k)
         def _():
             for d in range(1, PLANES):
                 z_copy(k, d).wait_send()
@@ -579,7 +538,6 @@
             pltpu.VMEM((2, 2, 4, 4, 64, 128), BF16),
             pltpu.VMEM((2, 2, 4, 64, 128), BF16),
             pltpu.VMEM((2, 2, 4, 4, 3, 16, 256), BF16),
-            pltpu.VMEM((3, 128, 128), F32),
             pltpu.VMEM((3, 2, 8, 16, 128), BF16),
             pltpu.VMEM((3, 8, 2, 16, 128), BF16),
             pltpu.VMEM((16, 32, 128), BF16),
@@ -591,11 +549,9 @@
             dma((2, 4)), dma((2, 4)),
             dma((2, 2)), dma((2, 2)),
             dma((2, 2)), dma((2, 2)),
-            dma((3, 2)), dma((3, 2)),
-            dma((2, 4)), dma((2, 2)),
+            dma((2, 2)), dma((2, 2)),
             pltpu.SemaphoreType.REGULAR,
             dma((2, 2)), dma((2, 2)),
-            dma, dma((2,)),
             dma((3, 7)), dma((3,)),
             dma((3,)), dma((3,)),
             dma((2,)), dma((2,)),

time: 44.4 us -> 43.8 us (0.986)
  the two profiles are of different devices: /device:TPU:32 before, /device:TPU:1 now
where the time goes in v5:
time: 43.8 us; the launch traced here: 43.7 us
  Pallas kernels  43.1 us (98%)
  between operations  0.64 us (1%)
    pallas_call x1, Pallas kernels, per_device(): pl.pallas_call(kernel, out_shape=(jax.ShapeDtypeStruct((16, 32, 128), BF1...  41.2 us
    pallas_call x1, Pallas kernels, per_device(): pl.pallas_call(assemble, out_shape=(jax.ShapeDtypeStruct((16, 2, 1024), F...  1.83 us

profile of v5, /device:TPU:1, one launch (start us, length us, event | category | flops | bytes accessed | tf_op | source)
XLA Modules:
  0.0 43.7 jit_solution(4802570833533565101)
XLA Ops:
  0.6 41.2 %shard_map.68 = (bf16[16,32,128]{2,1,0:T(8,128)(2,1)}, bf16[2,16,16,128]{3,2,1,0:T(8,128)(2,1)}) custom-call(bf16[2,3,16,2,16,512]{5,4,3,2,1,0:T(8,128)(2,1)} %bitcast.2, bf16[1536,1024]{1,0:T(8,128)(2,1)} %bitcast.3, bf16[2,3,16,512]{3,2,1,0:T(8,128)(2,1)} %lc.1, bf16[3,512,512]{2,1,0:T(8,128)(2,1)} %inv.1, f32[16,2,1024]{2,1,0:T(2,128)} %stat.1), custom_call_target="tpu_custom_call" | custom-call | flops 3400000000 | bytes 9000000 | tf_op jit(solution)/shard_map/pallas_call | solution.py:520
  41.9 1.8 %shard_map.69 = (f32[16,2,1024]{2,1,0:T(2,128)}, bf16[3,16,1024]{2,1,0:T(8,128)(2,1)}) custom-call(bf16[16,32,128]{2,1,0:T(8,128)(2,1)} %get-tuple-element.4.ug, bf16[2,16,16,128]{3,2,1,0:T(8,128)(2,1)} %get-tuple-element.5.xg), custom_call_target="tpu_custom_call" | custom-call | flops 200000 | bytes 500000 | tf_op jit(solution)/shard_map/pallas_call | solution.py:571
